TPU v7x, 256 devices: a whole 4x4x8 slice. The times are simulated.
256 devices in a mesh: tok: 16 (over x, y_hi, core), col: 8 (over z), grp: 2 (over y_lo).
Axes of the slice: x: 4, y: 4 (y_hi: 2, y_lo: 2; y = y_hi * 2 + y_lo), z: 8, core: 2. Of those that a mesh axis runs over, the one named last changes fastest.
Arguments:
- calibration: bfloat16 [24576, 4096], P(('tok', 'grp'), 'col'), may hold values from -1.1 to 1.1
- weight: float32 [4096, 4096], P(('tok', 'grp'), 'col'), may hold values from -6 to 6
- tile_mask: int32 [32, 32], P(('tok', 'grp'), 'col'), may hold values 0 or 1
- token_ids: int32 [2048], P(('tok', 'grp')), may hold values from 0 to 767
Outputs:
- new_weight: bfloat16 [4096, 4096], P(('tok', 'grp'), 'col')
- outputs: bfloat16 [2048, 4096], P('col', ('tok', 'grp'))
All inputs are finite; a program needn't handle non-finite values. No bound on the sum of `tile_mask` on one device may be relied on, other than what follows from the above.
Results may differ from a plain program's by a relative error of at most 0.0019.
The roundings to bfloat16 on the way count: a program that leaves them out, or rounds other values in their place, can miss the bound.
Values may be sent and summed in bfloat16 or wider, within the bound.
No kernel may reach another device: no remote copies, remote signals or barrier semaphores. Data moves between devices by JAX's collectives and lax.ppermute only.
A program may use at most 64 MiB of HBM per device.

v0:
```python
import jax
import jax.numpy as jnp
from jax import lax
from jax.sharding import PartitionSpec as P

TILE = 128
ITERS = 3
DAMPING = 0.1


def expand_tiles(tile_flags):
    tile_rows, tile_cols = tile_flags.shape
    expanded = jnp.broadcast_to(
        tile_flags.astype(jnp.float32)[:, None, :, None], (tile_rows, TILE, tile_cols, TILE)
    )
    return expanded.reshape(tile_rows * TILE, tile_cols * TILE)


def per_device(calibration, weight, tile_mask, token_ids):
    col_width = calibration.shape[1]
    col_count = lax.axis_size("col")
    width = col_width * col_count
    col_place = lax.axis_index("col")
    squares = jnp.sum(jnp.square(calibration.astype(jnp.float32)))
    trace_total = lax.psum(squares, ("tok", "col", "grp"))
    partial_gram = lax.dot_general(
        calibration,
        lax.all_gather(calibration, "col", axis=1, tiled=True),
        (((0,), (0,)), ((), ())),
        preferred_element_type=jnp.float32,
    )
    gram_slice = lax.psum_scatter(partial_gram, ("tok", "grp"), scatter_dimension=1, tiled=True)
    gram_rows = lax.all_gather(gram_slice, ("tok", "grp"), axis=1, tiled=True)
    trace_scale = trace_total / width
    row_ids = col_place * col_width + lax.broadcasted_iota(jnp.int32, gram_rows.shape, 0)
    col_ids = lax.broadcasted_iota(jnp.int32, gram_rows.shape, 1)
    stationary = gram_rows / trace_scale + jnp.where(row_ids == col_ids, DAMPING, 0.0)

    def apply_gram(operand):
        return lax.dot_general(
            lax.all_gather(operand, "col", axis=1, tiled=True),
            stationary,
            (((1,), (1,)), ((), ())),
            precision=lax.Precision.HIGHEST,
            preferred_element_type=jnp.float32,
        )

    keep_mask = expand_tiles(tile_mask)
    current = weight * keep_mask
    residual = apply_gram(current - weight)
    for iteration in range(ITERS):
        gradient = residual * keep_mask
        image_rows = apply_gram(gradient)
        sums_pair = lax.psum(
            (jnp.sum(gradient * gradient), jnp.sum(gradient * image_rows)), ("tok", "col", "grp")
        )
        length = sums_pair[0] / sums_pair[1]
        current = current - length * gradient
        if iteration + 1 < ITERS:
            residual = residual - length * image_rows
    new_weight = current.astype(jnp.bfloat16)
    chosen = jnp.take(calibration, token_ids, axis=0)
    all_chosen = lax.all_gather(chosen, ("tok", "grp"), axis=0, tiled=True)
    outputs = lax.psum_scatter(
        lax.dot_general(
            all_chosen, new_weight, (((1,), (1,)), ((), ())), preferred_element_type=jnp.float32
        ),
        "col",
        scatter_dimension=0,
        tiled=True,
    )
    return (new_weight, outputs.astype(jnp.bfloat16))


def solution(mesh):
    placed = (
        P(("tok", "grp"), "col"),
        P(("tok", "grp"), "col"),
        P(("tok", "grp"), "col"),
        P(("tok", "grp")),
    )
    return jax.shard_map(
        per_device,
        mesh=mesh,
        in_specs=placed,
        out_specs=(P(("tok", "grp"), "col"), P("col", ("tok", "grp"))),
        check_vma=False,
    )
```

profile of v0, /device:TPU:2, one launch (start us, length us, event | category | flops | bytes accessed | tf_op | source)
XLA Modules:
  0.0 833.4 jit_solution(12873526358352657317)
XLA Ops:
  7.9 79.3 %all-gather.10.cloned.1.call-done = bf16[768,4096]{1,0:T(8,128)(2,1)} async-done(((bf16[768,512]{1,0:T(8,128)(2,1)}), bf16[768,4096]{1,0:T(8,128)(2,1)}) %all-gather.10.cloned.1.call-update) | async-done | bytes 6291472 | tf_op jit(solution)/shard_map/all_gather | solution.py:28
  87.3 9.7 %fusion.4 = f32[512,4096]{1,0:T(8,128)} fusion(bf16[768,512]{1,0:T(8,128)(2,1)} %param.4, bf16[768,4096]{1,0:T(8,128)(2,1)} %all-gather.10.cloned.1.call-done), kind=kOutput, calls=%fused_computation.27 | convolution fusion | flops 3221225472 | bytes 15466496 | tf_op jit(solution)/shard_map/dot_general | solution.py:26
  97.1 143.3 %reduce-scatter.3.cloned.1.call-done = f32[512,128]{1,0:T(8,128)} async-done(((f32[512,4096]{1,0:T(8,128)}), f32[512,128]{1,0:T(8,128)}) %reduce-scatter.3.cloned.1.call-update) | async-done | bytes 262160 | tf_op jit(solution)/shard_map/reduce_scatter | solution.py:32
  240.6 0.7 multiply_subtract_fusion.1
  241.4 1.0 multiply_reduce_fusion
  242.4 77.8 %psum.49 = f32[]{:T(128)} all-reduce(f32[]{:T(128)} %multiply_reduce_fusion), channel_id=1, replica_groups=mesh['tok'=16,'col'=8,'grp'=2] {'tok','col','grp'}, use_global_device_ids=true, to_apply=%region_2.0 | all-reduce | flops 1 | bytes 8 | tf_op jit(solution)/shard_map/psum | solution.py:25
  320.8 22.7 %all-gather.12.cloned.1.call-done = f32[512,4096]{1,0:T(8,128)} async-done(((f32[512,128]{1,0:T(8,128)}), f32[512,4096]{1,0:T(8,128)}) %all-gather.12.cloned.1.call-update) | async-done | bytes 8388624 | tf_op jit(solution)/shard_map/all_gather | solution.py:33
  343.5 6.3 select_add_fusion
  349.8 36.7 %all-gather.8.cloned.1.call-done = f32[128,4096]{1,0:T(8,128)} async-done(((f32[128,512]{1,0:T(8,128)}), f32[128,4096]{1,0:T(8,128)}) %all-gather.8.cloned.1.call-update) | async-done | bytes 2097168 | tf_op jit(solution)/shard_map/all_gather | solution.py:41
  386.5 13.5 %broadcast_multiply_fusion.1 = (f32[128,512]{1,0:T(8,128)}, f32[128,512]{1,0:T(8,128)S(1)}) fusion(f32[512]{0:T(512)S(1)} %broadcast_bitcast_fusion, f32[128,4096]{1,0:T(8,128)} %all-gather.8.cloned.1.call-done, f32[512,4096]{1,0:T(8,128)} %select_add_fusion), kind=kOutput, calls=%fused_computation.19 | convolution fusion | flops 3221291008 | bytes 11012096 | tf_op jit(solution)/shard_map/dot_general | solution.py:40
  400.6 39.3 %all-gather.14.cloned.1.call-done = f32[128,4096]{1,0:T(8,128)} async-done(((f32[128,512]{1,0:T(8,128)}), f32[128,4096]{1,0:T(8,128)}) %all-gather.14.cloned.1.call-update) | async-done | bytes 2097168 | tf_op jit(solution)/shard_map/all_gather | solution.py:41
  439.8 13.4 %multiply_reduce_fusion.4 = (f32[]{:T(128)}, f32[]{:T(128)}, f32[128,512]{1,0:T(8,128)S(1)}) fusion(f32[128,512]{1,0:T(8,128)} %get-tuple-element.14, f32[128,4096]{1,0:T(8,128)} %all-gather.14.cloned.1.call-done, f32[512,4096]{1,0:T(8,128)} %select_add_fusion), kind=kOutput, calls=%fused_computation.16 | convolution fusion | flops 3221487616 | bytes 11010056 | tf_op jit(solution)/shard_map/dot_general | solution.py:40
  453.2 74.2 %all-reduce.2 = (f32[]{:T(128)}, f32[]{:T(128)}) all-reduce(f32[]{:T(128)} %get-tuple-element.5, f32[]{:T(128)} %get-tuple-element.4), channel_id=1, replica_groups=mesh['tok'=16,'col'=8,'grp'=2] {'tok','col','grp'}, use_global_device_ids=true, to_apply=%region_4.5 | all-reduce | flops 2 | bytes 16 | tf_op jit(solution)/shard_map/psum | solution.py:54
  528.7 0.8 broadcast_multiply_fusion
  529.8 37.6 %all-gather.16.cloned.1.call-done = f32[128,4096]{1,0:T(8,128)} async-done(((f32[128,512]{1,0:T(8,128)}), f32[128,4096]{1,0:T(8,128)}) %all-gather.16.cloned.1.call-update) | async-done | bytes 2097168 | tf_op jit(solution)/shard_map/all_gather | solution.py:41
  567.4 13.4 %multiply_reduce_fusion.2 = (f32[]{:T(128)}, f32[]{:T(128)}, f32[128,512]{1,0:T(8,128)S(1)}) fusion(f32[128,512]{1,0:T(8,128)} %broadcast_multiply_fusion, f32[128,4096]{1,0:T(8,128)} %all-gather.16.cloned.1.call-done, f32[512,4096]{1,0:T(8,128)} %select_add_fusion), kind=kOutput, calls=%fused_computation.13 | convolution fusion | flops 3221487616 | bytes 11010056 | tf_op jit(solution)/shard_map/dot_general | solution.py:40
  580.8 74.2 %all-reduce.1 = (f32[]{:T(128)}, f32[]{:T(128)}) all-reduce(f32[]{:T(128)} %get-tuple-element.3, f32[]{:T(128)} %get-tuple-element.2), channel_id=1, replica_groups=mesh['tok'=16,'col'=8,'grp'=2] {'tok','col','grp'}, use_global_device_ids=true, to_apply=%region_8.9 | all-reduce | flops 2 | bytes 16 | tf_op jit(solution)/shard_map/psum | solution.py:54
  656.3 1.4 multiply_reduce_fusion.1
  659.6 36.1 %all-gather.18.cloned.1.call-done = f32[128,4096]{1,0:T(8,128)} async-done(((f32[128,512]{1,0:T(8,128)}), f32[128,4096]{1,0:T(8,128)}) %all-gather.18.cloned.1.call-update) | async-done | bytes 2097168 | tf_op jit(solution)/shard_map/all_gather | solution.py:41
  695.7 13.4 %fusion = f32[]{:T(128)} fusion(f32[128,512]{1,0:T(8,128)} %get-tuple-element.13, f32[128,4096]{1,0:T(8,128)} %all-gather.18.cloned.1.call-done, f32[512,4096]{1,0:T(8,128)} %select_add_fusion), kind=kOutput, calls=%fused_computation.5 | convolution fusion | flops 3221356544 | bytes 10747908 | tf_op jit(solution)/shard_map/dot_general | solution.py:40
  709.0 74.2 %all-reduce = (f32[]{:T(128)}, f32[]{:T(128)}) all-reduce(f32[]{:T(128)} %get-tuple-element.12, f32[]{:T(128)} %fusion), channel_id=1, replica_groups=mesh['tok'=16,'col'=8,'grp'=2] {'tok','col','grp'}, use_global_device_ids=true, to_apply=%region_12.13 | all-reduce | flops 2 | bytes 16 | tf_op jit(solution)/shard_map/psum | solution.py:54
  784.8 3.3 fusion.5
  788.1 37.0 %reduce-scatter.5.cloned.1.call-done = f32[256,128]{1,0:T(8,128)} async-done(((f32[2048,128]{1,0:T(8,128)}), f32[256,128]{1,0:T(8,128)}) %reduce-scatter.5.cloned.1.call-update) | async-done | bytes 131088 | tf_op jit(solution)/shard_map/reduce_scatter | solution.py:64
  825.1 1.5 convert_element_type.15
  (44 shorter events, 3.8 us)
Async XLA Ops:
  7.2 80.1 %all-gather.10.cloned.1.call-start = ((), (), s32[]{:S(2)}) async-start(), calls=%async_computation.3 | async-start | bytes 7077888 | tf_op jit(solution)/shard_map/all_gather | solution.py:28
  7.9 232.5 %reduce-scatter.3.cloned.1.call-start = ((), (), s32[]{:S(2)}) async-start(), calls=%async_computation.4 | async-start | bytes 8650752 | tf_op jit(solution)/shard_map/reduce_scatter | solution.py:32
  97.0 143.5 %copy-start.6 = (s32[1,4]{1,0:T(1,128)S(1)}, s32[1,4]{1,0:T(1,128)}, u32[]{:S(2)}) copy-start(s32[1,4]{1,0:T(1,128)} %param.6) | copy-start | bytes 52
  97.0 143.6 %copy-start.4 = (f32[128,512]{1,0:T(8,128)S(1)}, f32[128,512]{1,0:T(8,128)}, u32[]{:S(2)}) copy-start(f32[128,512]{1,0:T(8,128)} %param.5) | copy-start | bytes 786436
  97.0 144.4 %copy-start = (bf16[768,512]{1,0:T(8,128)(2,1)S(1)}, bf16[768,512]{1,0:T(8,128)(2,1)}, u32[]{:S(2)}) copy-start(bf16[768,512]{1,0:T(8,128)(2,1)} %param.4) | copy-start | bytes 2359300
  97.0 246.5 %all-gather.12.cloned.1.call-start = ((), (), s32[]{:S(2)}) async-start(), calls=%async_computation.5 | async-start | bytes 8650752 | tf_op jit(solution)/shard_map/all_gather | solution.py:33
  240.4 146.1 %all-gather.8.cloned.1.call-start = ((), (), s32[]{:S(2)}) async-start(), calls=%async_computation.2 | async-start | bytes 2359296 | tf_op jit(solution)/shard_map/all_gather | solution.py:41
  241.3 198.5 %all-gather.14.cloned.1.call-start = ((), (), s32[]{:S(2)}) async-start(), calls=%async_computation.6 | async-start | bytes 2359296 | tf_op jit(solution)/shard_map/all_gather | solution.py:41
  400.0 167.4 %all-gather.16.cloned.1.call-start = ((), (), s32[]{:S(2)}) async-start(), calls=%async_computation.7 | async-start | bytes 2359296 | tf_op jit(solution)/shard_map/all_gather | solution.py:41
  529.5 128.3 %copy-start.7 = (s32[64]{0:T(128)S(1)}, s32[64]{0:T(128)}, u32[]{:S(2)}) copy-start(s32[64]{0:T(128)} %param.7) | copy-start | bytes 772
  529.5 166.1 %all-gather.18.cloned.1.call-start = ((), (), s32[]{:S(2)}) async-start(), calls=%async_computation.8 | async-start | bytes 2359296 | tf_op jit(solution)/shard_map/all_gather | solution.py:41
  656.3 128.3 %copy-start.1 = (f32[128,512]{1,0:T(8,128)S(1)}, f32[128,512]{1,0:T(8,128)}, u32[]{:S(2)}) copy-start(f32[128,512]{1,0:T(8,128)} %get-tuple-element.14) | copy-start | bytes 786436
  656.3 128.3 %copy-start.3 = (f32[128,512]{1,0:T(8,128)S(1)}, f32[128,512]{1,0:T(8,128)}, u32[]{:S(2)}) copy-start(f32[128,512]{1,0:T(8,128)} %broadcast_multiply_fusion) | copy-start | bytes 786436
  657.7 126.9 %copy-start.2 = (f32[128,512]{1,0:T(8,128)S(1)}, f32[128,512]{1,0:T(8,128)}, u32[]{:S(2)}) copy-start(f32[128,512]{1,0:T(8,128)} %get-tuple-element.13) | copy-start | bytes 786436
  657.8 127.0 %all-gather.20.cloned.1.call-start = ((), (), s32[]{:S(2)}) async-start(), calls=%async_computation.9 | async-start | bytes 2162688 | tf_op jit(solution)/shard_map/all_gather | solution.py:63
  659.3 165.8 %reduce-scatter.5.cloned.1.call-start = ((), (), s32[]{:S(2)}) async-start(), calls=%async_computation.10 | async-start | bytes 1179648 | tf_op jit(solution)/shard_map/reduce_scatter | solution.py:64
  784.8 41.9 %copy-start.5 = (bf16[128,512]{1,0:T(8,128)(2,1)}, bf16[128,512]{1,0:T(8,128)(2,1)S(1)}, u32[]{:S(2)}) copy-start(bf16[128,512]{1,0:T(8,128)(2,1)S(1)} %fusion.3) | copy-start | bytes 393220
Sparse Core Ops, SparseCore 0:
  9.8 77.4 all-gather.9
  97.2 143.1 reduce-scatter.2
  242.1 101.3 all-gather.11
  345.2 41.3 all-gather.7
  400.1 39.6 all-gather.13
  529.7 37.7 all-gather.15
  657.9 37.7 all-gather.17
  698.0 84.5 all-gather.19
  788.3 36.8 reduce-scatter.4
where the time goes:
time: 838 us; the launch traced here: 833 us
  waiting for transfers between devices  433 us (52%)
  blocking collectives  300 us (36%)
  matrix products  66.6 us (8%)
  between operations  18.9 us (2%)
  other arithmetic  12.6 us (2%)
    psum x3, blocking collectives, per_device(): lax.psum((jnp.sum(gradient * gradient), jnp.sum(gradient * image_rows)),...  223 us
    all_gather x4, waiting for transfers between devices, apply_gram(): lax.all_gather(operand, 'col', axis=1, tiled=True)  150 us
    reduce_scatter x1, waiting for transfers between devices, per_device(): lax.psum_scatter(partial_gram, ('tok', 'grp'), scatter_dimension=1, tiled...  143 us
    all_gather x1, waiting for transfers between devices, per_device(): lax.all_gather(calibration, 'col', axis=1, tiled=True)  79.3 us
    psum x1, blocking collectives, per_device(): trace_total = lax.psum(squares, ('tok', 'col', 'grp'))  77.8 us
    dot_general x4, matrix products, apply_gram(): lax.dot_general(lax.all_gather(operand, 'col', axis=1, tiled=True), stati...  53.5 us
    reduce_scatter x1, waiting for transfers between devices, per_device(): lax.psum_scatter(lax.dot_general(all_chosen, new_weight, (((1,), (1,)), (...  37 us
    all_gather x1, waiting for transfers between devices, per_device(): gram_rows = lax.all_gather(gram_slice, ('tok', 'grp'), axis=1, tiled=True)  22.7 us
  transfers between devices with their start and end apart: 9, of which 8 were waited for; matrix products, arithmetic and copies ran while one was open for 3% of the time, Pallas kernels for 0%

commit v1 on v0

--- a/solution.py
+++ b/solution.py
@@ -25,7 +25,9 @@
     trace_total = lax.psum(squares, ("tok", "col", "grp"))
     partial_gram = lax.dot_general(
         calibration,
-        lax.all_gather(calibration, "col", axis=1, tiled=True),
+        jnp.concatenate(
+            lax.all_to_all(jnp.stack([calibration] * lax.axis_size("col")), "col", 0, 0), axis=1
+        ),
         (((0,), (0,)), ((), ())),
         preferred_element_type=jnp.float32,
     )

time: 838 us -> 908 us (1.084)
  blocking collectives: 300 us -> 450 us
  waiting for transfers between devices: 433 us -> 351 us
    all_to_all x0 -> x1, blocking collectives: none -> 149 us  [per_device(): lax.all_to_all(jnp.stack([calibration] * lax.axis_size('col')), 'col', 0, 0)]
    all_gather x1 -> x0, waiting for transfers between devices: 79.3 us -> none  [per_device(): lax.all_gather(calibration, 'col', axis=1, tiled=True)]
  transfers between devices with their start and end apart: 9 -> 8, of which waited for: 8 -> 7; matrix products, arithmetic and copies ran while one was open for 3% -> 3% of each run, Pallas kernels for 0% -> 0%
where the time goes in v1:
time: 908 us; the launch traced here: 898 us
  blocking collectives  450 us (50%)
  waiting for transfers between devices  351 us (39%)
  matrix products  62.5 us (7%)
  between operations  19.1 us (2%)
  other arithmetic  12.6 us (1%)
    psum x3, blocking collectives, per_device(): lax.psum((jnp.sum(gradient * gradient), jnp.sum(gradient * image_rows)),...  223 us
    all_gather x4, waiting for transfers between devices, apply_gram(): lax.all_gather(operand, 'col', axis=1, tiled=True)  150 us
    all_to_all x1, blocking collectives, per_device(): lax.all_to_all(jnp.stack([calibration] * lax.axis_size('col')), 'col', 0, 0)  149 us
    reduce_scatter x1, waiting for transfers between devices, per_device(): lax.psum_scatter(partial_gram, ('tok', 'grp'), scatter_dimension=1, tiled...  141 us
    psum x1, blocking collectives, per_device(): trace_total = lax.psum(squares, ('tok', 'col', 'grp'))  77.4 us
    dot_general x4, matrix products, apply_gram(): lax.dot_general(lax.all_gather(operand, 'col', axis=1, tiled=True), stati...  53.5 us
    reduce_scatter x1, waiting for transfers between devices, per_device(): lax.psum_scatter(lax.dot_general(all_chosen, new_weight, (((1,), (1,)), (...  36.9 us
    all_gather x1, waiting for transfers between devices, per_device(): gram_rows = lax.all_gather(gram_slice, ('tok', 'grp'), axis=1, tiled=True)  22.9 us
  transfers between devices with their start and end apart: 8, of which 7 were waited for; matrix products, arithmetic and copies ran while one was open for 3% of the time, Pallas kernels for 0%

profile of v1, /device:TPU:2, one launch (start us, length us, event | category | flops | bytes accessed | tf_op | source)
XLA Modules:
  0.0 898.4 jit_solution(10332964519267958768)
XLA Ops:
  7.2 1.4 copy.6
  9.0 149.5 %all_to_all.5 = bf16[8,768,512]{1,2,0:T(8,128)(2,1)S(1)} all-to-all(bf16[8,768,512]{1,2,0:T(8,128)(2,1)S(1)} %stack.2), channel_id=1, replica_groups=mesh['tok'=16,'col'=8,'grp'=2] {'col'}, dimensions={0} | all-to-all | bytes 12582912 | tf_op jit(solution)/shard_map/all_to_all | solution.py:29
  158.5 5.7 fusion.4
  164.3 141.0 %reduce-scatter.3.cloned.1.call-done = f32[512,128]{1,0:T(8,128)} async-done(((f32[512,4096]{1,0:T(8,128)}), f32[512,128]{1,0:T(8,128)}) %reduce-scatter.3.cloned.1.call-update) | async-done | bytes 262160 | tf_op jit(solution)/shard_map/reduce_scatter | solution.py:34
  306.3 1.0 multiply_reduce_fusion
  307.3 77.4 %psum.49 = f32[]{:T(128)} all-reduce(f32[]{:T(128)} %multiply_reduce_fusion), channel_id=1, replica_groups=mesh['tok'=16,'col'=8,'grp'=2] {'tok','col','grp'}, use_global_device_ids=true, to_apply=%region_2.0 | all-reduce | flops 1 | bytes 8 | tf_op jit(solution)/shard_map/psum | solution.py:25
  385.3 22.9 %all-gather.9.cloned.1.call-done = f32[512,4096]{1,0:T(8,128)} async-done(((f32[512,128]{1,0:T(8,128)}), f32[512,4096]{1,0:T(8,128)}) %all-gather.9.cloned.1.call-update) | async-done | bytes 8388624 | tf_op jit(solution)/shard_map/all_gather | solution.py:35
  408.2 6.3 select_add_fusion
  414.5 36.8 %all-gather.7.cloned.1.call-done = f32[128,4096]{1,0:T(8,128)} async-done(((f32[128,512]{1,0:T(8,128)}), f32[128,4096]{1,0:T(8,128)}) %all-gather.7.cloned.1.call-update) | async-done | bytes 2097168 | tf_op jit(solution)/shard_map/all_gather | solution.py:43
  451.3 13.5 %broadcast_multiply_fusion.1 = (f32[128,512]{1,0:T(8,128)}, f32[128,512]{1,0:T(8,128)S(1)}) fusion(f32[512]{0:T(512)S(1)} %broadcast_bitcast_fusion, f32[128,4096]{1,0:T(8,128)} %all-gather.7.cloned.1.call-done, f32[512,4096]{1,0:T(8,128)} %select_add_fusion), kind=kOutput, calls=%fused_computation.19 | convolution fusion | flops 3221291008 | bytes 11012096 | tf_op jit(solution)/shard_map/dot_general | solution.py:42
  465.3 39.3 %all-gather.11.cloned.1.call-done = f32[128,4096]{1,0:T(8,128)} async-done(((f32[128,512]{1,0:T(8,128)}), f32[128,4096]{1,0:T(8,128)}) %all-gather.11.cloned.1.call-update) | async-done | bytes 2097168 | tf_op jit(solution)/shard_map/all_gather | solution.py:43
  504.6 13.3 %multiply_reduce_fusion.4 = (f32[]{:T(128)}, f32[]{:T(128)}, f32[128,512]{1,0:T(8,128)S(1)}) fusion(f32[128,512]{1,0:T(8,128)} %get-tuple-element.14, f32[128,4096]{1,0:T(8,128)} %all-gather.11.cloned.1.call-done, f32[512,4096]{1,0:T(8,128)} %select_add_fusion), kind=kOutput, calls=%fused_computation.16 | convolution fusion | flops 3221487616 | bytes 11010056 | tf_op jit(solution)/shard_map/dot_general | solution.py:42
  518.0 74.2 %all-reduce.2 = (f32[]{:T(128)}, f32[]{:T(128)}) all-reduce(f32[]{:T(128)} %get-tuple-element.5, f32[]{:T(128)} %get-tuple-element.4), channel_id=1, replica_groups=mesh['tok'=16,'col'=8,'grp'=2] {'tok','col','grp'}, use_global_device_ids=true, to_apply=%region_4.5 | all-reduce | flops 2 | bytes 16 | tf_op jit(solution)/shard_map/psum | solution.py:56
  593.5 0.8 broadcast_multiply_fusion
  594.6 37.6 %all-gather.13.cloned.1.call-done = f32[128,4096]{1,0:T(8,128)} async-done(((f32[128,512]{1,0:T(8,128)}), f32[128,4096]{1,0:T(8,128)}) %all-gather.13.cloned.1.call-update) | async-done | bytes 2097168 | tf_op jit(solution)/shard_map/all_gather | solution.py:43
  632.2 13.4 %multiply_reduce_fusion.2 = (f32[]{:T(128)}, f32[]{:T(128)}, f32[128,512]{1,0:T(8,128)S(1)}) fusion(f32[128,512]{1,0:T(8,128)} %broadcast_multiply_fusion, f32[128,4096]{1,0:T(8,128)} %all-gather.13.cloned.1.call-done, f32[512,4096]{1,0:T(8,128)} %select_add_fusion), kind=kOutput, calls=%fused_computation.13 | convolution fusion | flops 3221487616 | bytes 11010056 | tf_op jit(solution)/shard_map/dot_general | solution.py:42
  645.6 74.2 %all-reduce.1 = (f32[]{:T(128)}, f32[]{:T(128)}) all-reduce(f32[]{:T(128)} %get-tuple-element.3, f32[]{:T(128)} %get-tuple-element.2), channel_id=1, replica_groups=mesh['tok'=16,'col'=8,'grp'=2] {'tok','col','grp'}, use_global_device_ids=true, to_apply=%region_8.9 | all-reduce | flops 2 | bytes 16 | tf_op jit(solution)/shard_map/psum | solution.py:56
  721.2 1.4 multiply_reduce_fusion.1
  724.4 36.1 %all-gather.15.cloned.1.call-done = f32[128,4096]{1,0:T(8,128)} async-done(((f32[128,512]{1,0:T(8,128)}), f32[128,4096]{1,0:T(8,128)}) %all-gather.15.cloned.1.call-update) | async-done | bytes 2097168 | tf_op jit(solution)/shard_map/all_gather | solution.py:43
  760.5 13.3 %fusion = f32[]{:T(128)} fusion(f32[128,512]{1,0:T(8,128)} %get-tuple-element.13, f32[128,4096]{1,0:T(8,128)} %all-gather.15.cloned.1.call-done, f32[512,4096]{1,0:T(8,128)} %select_add_fusion), kind=kOutput, calls=%fused_computation.5 | convolution fusion | flops 3221356544 | bytes 10747908 | tf_op jit(solution)/shard_map/dot_general | solution.py:42
  773.8 74.2 %all-reduce = (f32[]{:T(128)}, f32[]{:T(128)}) all-reduce(f32[]{:T(128)} %get-tuple-element.12, f32[]{:T(128)} %fusion), channel_id=1, replica_groups=mesh['tok'=16,'col'=8,'grp'=2] {'tok','col','grp'}, use_global_device_ids=true, to_apply=%region_12.13 | all-reduce | flops 2 | bytes 16 | tf_op jit(solution)/shard_map/psum | solution.py:56
  849.5 3.3 fusion.5
  852.8 36.9 %reduce-scatter.5.cloned.1.call-done = f32[256,128]{1,0:T(8,128)} async-done(((f32[2048,128]{1,0:T(8,128)}), f32[256,128]{1,0:T(8,128)}) %reduce-scatter.5.cloned.1.call-update) | async-done | bytes 131088 | tf_op jit(solution)/shard_map/reduce_scatter | solution.py:66
  889.8 1.5 convert_element_type.15
  (44 shorter events, 4.2 us)
Async XLA Ops:
  7.2 298.2 %reduce-scatter.3.cloned.1.call-start = ((), (), s32[]{:S(2)}) async-start(), calls=%async_computation.4 | async-start | bytes 8650752 | tf_op jit(solution)/shard_map/reduce_scatter | solution.py:34
  9.0 149.5 %copy-start = (bf16[768,512]{1,0:T(8,128)(2,1)S(1)}, bf16[768,512]{1,0:T(8,128)(2,1)}, u32[]{:S(2)}) copy-start(bf16[768,512]{1,0:T(8,128)(2,1)} %param.4) | copy-start | bytes 2359300
  164.2 141.2 %copy-start.6 = (s32[1,4]{1,0:T(1,128)S(1)}, s32[1,4]{1,0:T(1,128)}, u32[]{:S(2)}) copy-start(s32[1,4]{1,0:T(1,128)} %param.6) | copy-start | bytes 52
  164.2 141.3 %copy-start.4 = (f32[128,512]{1,0:T(8,128)S(1)}, f32[128,512]{1,0:T(8,128)}, u32[]{:S(2)}) copy-start(f32[128,512]{1,0:T(8,128)} %param.5) | copy-start | bytes 786436
  164.2 244.0 %all-gather.9.cloned.1.call-start = ((), (), s32[]{:S(2)}) async-start(), calls=%async_computation.5 | async-start | bytes 8650752 | tf_op jit(solution)/shard_map/all_gather | solution.py:35
  305.3 146.0 %all-gather.7.cloned.1.call-start = ((), (), s32[]{:S(2)}) async-start(), calls=%async_computation.3 | async-start | bytes 2359296 | tf_op jit(solution)/shard_map/all_gather | solution.py:43
  306.3 198.4 %all-gather.11.cloned.1.call-start = ((), (), s32[]{:S(2)}) async-start(), calls=%async_computation.6 | async-start | bytes 2359296 | tf_op jit(solution)/shard_map/all_gather | solution.py:43
  464.8 167.4 %all-gather.13.cloned.1.call-start = ((), (), s32[]{:S(2)}) async-start(), calls=%async_computation.7 | async-start | bytes 2359296 | tf_op jit(solution)/shard_map/all_gather | solution.py:43
  594.3 128.3 %copy-start.7 = (s32[64]{0:T(128)S(1)}, s32[64]{0:T(128)}, u32[]{:S(2)}) copy-start(s32[64]{0:T(128)} %param.7) | copy-start | bytes 772
  594.3 166.1 %all-gather.15.cloned.1.call-start = ((), (), s32[]{:S(2)}) async-start(), calls=%async_computation.8 | async-start | bytes 2359296 | tf_op jit(solution)/shard_map/all_gather | solution.py:43
  721.1 128.2 %copy-start.1 = (f32[128,512]{1,0:T(8,128)S(1)}, f32[128,512]{1,0:T(8,128)}, u32[]{:S(2)}) copy-start(f32[128,512]{1,0:T(8,128)} %get-tuple-element.14) | copy-start | bytes 786436
  721.1 128.2 %copy-start.3 = (f32[128,512]{1,0:T(8,128)S(1)}, f32[128,512]{1,0:T(8,128)}, u32[]{:S(2)}) copy-start(f32[128,512]{1,0:T(8,128)} %broadcast_multiply_fusion) | copy-start | bytes 786436
  722.6 126.8 %copy-start.2 = (f32[128,512]{1,0:T(8,128)S(1)}, f32[128,512]{1,0:T(8,128)}, u32[]{:S(2)}) copy-start(f32[128,512]{1,0:T(8,128)} %get-tuple-element.13) | copy-start | bytes 786436
  722.6 126.9 %all-gather.17.cloned.1.call-start = ((), (), s32[]{:S(2)}) async-start(), calls=%async_computation.9 | async-start | bytes 2162688 | tf_op jit(solution)/shard_map/all_gather | solution.py:65
  724.1 165.6 %reduce-scatter.5.cloned.1.call-start = ((), (), s32[]{:S(2)}) async-start(), calls=%async_computation.10 | async-start | bytes 1179648 | tf_op jit(solution)/shard_map/reduce_scatter | solution.py:66
  849.5 41.8 %copy-start.5 = (bf16[128,512]{1,0:T(8,128)(2,1)}, bf16[128,512]{1,0:T(8,128)(2,1)S(1)}, u32[]{:S(2)}) copy-start(bf16[128,512]{1,0:T(8,128)(2,1)S(1)} %fusion.3) | copy-start | bytes 393220
Sparse Core Ops, SparseCore 0:
  164.3 140.9 reduce-scatter.2
  307.1 101.1 all-gather.8
  410.0 41.2 all-gather.6
  464.9 39.6 all-gather.10
  594.5 37.7 all-gather.12
  722.7 37.7 all-gather.14
  762.9 84.5 all-gather.16
  853.0 36.7 reduce-scatter.4
